TPU v7x, 128 devices: a whole 4x4x4 slice. The times are simulated.
128 devices in a mesh: fn: 4 (over z), se: 32 (over x, y, core).
Axes of the slice: x: 4, y: 4, z: 4, core: 2. Of those that a mesh axis runs over, the one named last changes fastest.
Arguments:
- iface_adj: bfloat16 [384, 98304], P(('fn', 'se')), may hold values from -6 to 6
- panels: bfloat16 [512, 1536, 1536], P('se', 'fn'), may hold values from -0.15625 to 0.15625
- block_mask: int32 [512, 16, 16], P('se', 'fn'), may hold values 0 or 1
- connectivity: int32 [512, 16], P('se'), may hold values from 0 to 31, as said below
- var_map: int32 [512, 16], P('se', 'fn'), may hold values from 0 to 2047
- state_terms: float32 [512, 1536], P('se', 'fn'), may hold values from -0.24 to 0.24
Outputs:
- interior_adj: bfloat16 [512, 384, 1536], P('se', None, 'fn')
- thickness_grad: float32 [384, 2048], P(('fn', 'se'))
Inputs may be any that keep to these rules, and one draw needn't show every extreme that they name: `connectivity`: each row names 16 different interface blocks of its own group.
All inputs are finite; a program needn't handle non-finite values. No bound on the sum of `block_mask` on one device may be relied on, other than what follows from the above.
Results may differ from a plain program's by a relative error of at most 0.001.
Values may be sent and summed in bfloat16 or wider, within the bound.
A program may use at most 192 MiB of HBM per device.

v0:
```python
import jax
import jax.numpy as jnp
from jax import lax
from jax.sharding import PartitionSpec as P

NB = 96
NBLK = 16
NV = 2048


def body(iface_adj, panels, block_mask, connectivity, var_map, state_terms):
    at_owner = lax.all_to_all(iface_adj, "se", split_axis=1, concat_axis=0, tiled=True)
    local_count, row_count, full_order = panels.shape
    row_blocks = row_count // NB
    blocks = (
        panels.reshape(local_count, row_blocks, NB, NBLK, NB)
        * block_mask.astype(panels.dtype)[:, :, None, :, None]
    )
    blocks = blocks.reshape(local_count, row_count, full_order)
    fn_piece = lax.all_gather(at_owner, "fn", axis=0, tiled=True)
    how_many = fn_piece.shape[0]
    boundary = jnp.take(fn_piece.reshape(how_many, -1, NB), connectivity, axis=1)
    boundary = boundary.reshape(how_many, local_count, full_order)
    interior = -jnp.einsum("fsm,srm->sfr", boundary, blocks, preferred_element_type=jnp.float32)
    func_count = interior.shape[1]
    weights = state_terms.reshape(local_count, 1, row_blocks, NB)
    block_sums = jnp.sum(
        interior.reshape(local_count, func_count, row_blocks, NB) * weights, axis=3
    )
    onehot = (var_map[:, :, None] == jnp.arange(NV, dtype=jnp.int32)[None, None, :]).astype(
        jnp.float32
    )
    gradient = lax.psum_scatter(
        jnp.einsum("sfb,sbv->fv", block_sums, onehot, precision=lax.Precision.HIGHEST),
        ("fn", "se"),
        scatter_dimension=0,
        tiled=True,
    )
    return (interior.astype(jnp.bfloat16), gradient)


def solution(mesh):
    placed = (
        P(("fn", "se"), None),
        P("se", "fn", None),
        P("se", "fn", None),
        P("se", None),
        P("se", "fn"),
        P("se", "fn"),
    )
    return jax.shard_map(
        body,
        mesh=mesh,
        in_specs=placed,
        out_specs=(P("se", None, "fn"), P(("fn", "se"), None)),
        check_vma=False,
    )
```

profile of v0, /device:TPU:1, one launch (start us, length us, event | category | flops | bytes accessed | tf_op | source)
XLA Modules:
  0.0 290.1 jit_solution(3615746930722943804)
XLA Ops:
  7.2 0.0 all-gather.2.cloned.1.call-start
  7.2 22.8 %all_to_all.19 = bf16[3,32,3072]{2,0,1:T(4,128)(2,1)S(1)} all-to-all(bf16[3,32,3072]{2,0,1:T(4,128)(2,1)} %bitcast.17), channel_id=1, replica_groups=mesh['fn'=4,'se'=32] {'se'}, dimensions={1} | all-to-all | bytes 1179648 | tf_op jit(solution)/shard_map/all_to_all | solution.py:12
  30.0 1.2 all_to_all.17
  31.2 0.0 all-gather.2.cloned.1.call-update
  31.3 0.0 all-reduce.3.cloned.1.call-start
  31.3 0.8 convert_element_type.7
  32.1 8.7 %mul.21 = bf16[16,4,96,16,96]{4,3,2,1,0:T(8,128)(2,1)} broadcast(bf16[16,4,16]{2,1,0:T(4,128)(2,1)S(1)} %convert_element_type.7), dimensions={0,1,3} | broadcast | bytes 18876416 | tf_op jit(solution)/shard_map/mul | solution.py:16
  40.8 0.0 copy-start
  40.8 0.0 copy-start.1
  40.8 41.3 %mul.22 = bf16[16,384,1536]{2,1,0:T(8,128)(2,1)} reshape(bf16[16,4,96,16,96]{4,3,2,1,0:T(8,128)(2,1)} %mul.21) | data formatting | bytes 37748736 | tf_op jit(solution)/shard_map/mul | solution.py:16
  82.2 0.0 copy-done
  82.2 0.1 reshape.32
  82.3 0.1 broadcast_in_dim.19
  82.4 0.1 broadcast_in_dim.20
  82.5 0.0 copy-done.1
  82.5 0.1 mul.24
  82.6 0.0 all-gather.2.cloned.1.call-done
  82.6 3.0 %copy.14 = bf16[384,3072]{0,1:T(8,128)(2,1)S(1)} copy(bf16[384,3072]{1,0:T(8,128)(2,1)} %all-gather.2.cloned.1.call-done) | data formatting | bytes 4718592 | tf_op jit(solution)/shard_map/all_gather | solution.py:20
  85.6 11.2 %gather_fusion = bf16[256,384,96]{1,2,0:T(8,128)(2,1)} fusion(bf16[384,32,96]{0,2,1:T(8,128)(2,1)S(1)} %bitcast.13, s32[1024]{0:T(1024)S(1)} %pad_clamp_fusion), kind=kCustom, calls=%fused_computation | custom fusion | bytes 37749760 | tf_op jit(solution)/shard_map/jit(_take)/gather | solution.py:22
  96.9 0.0 copy-start.2
  96.9 25.0 %fusion.13 = (bf16[16,384,384]{1,2,0:T(8,128)(2,1)}, f32[16,384,384]{1,2,0:T(8,128)}) fusion(bf16[384,16,1536]{0,2,1:T(8,128)(2,1)} %bitcast.14, pred[16,1536]{1,0:T(8,128)(4,1)S(1)} %broadcast_in_dim.20, bf16[16,384,1536]{2,1,0:T(8,128)(2,1)} %param.7, bf16[16,384,1536]{2,1,0:T(8,128)(2,1)} %mul.22), kind=kOutput, calls=%fused_computation.17 | convolution fusion | flops 7299661824 | bytes 70803456 | tf_op jit(solution)/shard_map/fsm,srm->sfr/dot_general | solution.py:24
  121.9 5.1 %multiply_reduce_fusion = f32[16,384,4]{1,2,0:T(4,128)S(1)} fusion(f32[16,384,4,96]{1,3,2,0:T(8,128)} %bitcast.15, f32[16,4,96]{2,1,0:T(4,128)S(1)} %mul.24), kind=kLoop, calls=%fused_computation.5 | loop fusion | flops 4694016 | bytes 9560064 | tf_op jit(solution)/shard_map/reduce_sum | solution.py:27
  127.0 0.0 copy-done.2
  127.0 3.1 %convolution_bitcast_fusion = f32[384,2048]{1,0:T(8,128)} fusion(s32[16,4]{0,1:T(4,128)S(1)} %copy-done.2, f32[16,384,4]{1,2,0:T(4,128)S(1)} %multiply_reduce_fusion), kind=kOutput, calls=%fused_computation.8 | convolution fusion | flops 604110848 | bytes 3244288 | tf_op jit(solution)/shard_map/sfb,sbv->fv/dot_general | solution.py:34
  130.1 0.0 all-reduce.3.cloned.1.call-update
  130.2 6.6 %copy.17 = bf16[16,384,384]{2,1,0:T(8,128)(2,1)} copy(bf16[16,384,384]{1,2,0:T(8,128)(2,1)} %get-tuple-element.8) | data formatting | bytes 9437184
  136.8 145.0 %all-reduce.3.cloned.1.call-done = f32[384,2048]{1,0:T(8,128)} async-done(((f32[384,2048]{1,0:T(8,128)}), f32[384,2048]{1,0:T(8,128)}) %all-reduce.3.cloned.1.call-update) | async-done | bytes 3145744
  281.8 1.5 constant_dynamic-slice_fusion
  (3 shorter events, 0.0 us)
Async XLA Ops:
  7.2 75.5 %all-gather.2.cloned.1.call-start = ((), (), s32[]{:S(2)}) async-start(), calls=%async_computation.1 | async-start | bytes 2949120 | tf_op jit(solution)/shard_map/all_gather | solution.py:20
  31.3 250.5 %all-reduce.3.cloned.1.call-start = ((), (), s32[]{:S(2)}) async-start(), calls=%async_computation.2 | async-start | bytes 6291456
  40.8 41.3 %copy-start = (s32[16,16]{1,0:T(8,128)S(1)}, s32[16,16]{1,0:T(8,128)}, u32[]{:S(2)}) copy-start(s32[16,16]{1,0:T(8,128)} %param.9) | copy-start | bytes 3076
  40.8 41.7 %copy-start.1 = (f32[16,384]{1,0:T(8,128)S(1)}, f32[16,384]{1,0:T(8,128)}, u32[]{:S(2)}) copy-start(f32[16,384]{1,0:T(8,128)} %param.11) | copy-start | bytes 73732
  96.9 30.1 %copy-start.2 = (s32[16,4]{0,1:T(4,128)S(1)}, s32[16,4]{0,1:T(4,128)}, u32[]{:S(2)}) copy-start(s32[16,4]{0,1:T(4,128)} %param.10) | copy-start | bytes 772
Sparse Core Ops, SparseCore 0:
  31.4 31.6 all-gather.1
  130.3 151.4 all-reduce.2
where the time goes:
time: 292 us; the launch traced here: 290 us
  waiting for transfers between devices  145 us (50%)
  local copies, waits for them, and re-layouts  74.1 us (25%)
  matrix products  28.1 us (10%)
  blocking collectives  22.8 us (8%)
  between operations  14.1 us (5%)
  other arithmetic  5.89 us (2%)
    unnamed x3, waiting for transfers between devices  145 us
    mul x2, local copies, waits for them, and re-layouts, body(): panels.reshape(local_count, row_blocks, NB, NBLK, NB)  50.1 us
    dot_general x1, matrix products, body(): jnp.einsum('fsm,srm->sfr', boundary, blocks, preferred_element_type=jnp.f...  25 us
    all_to_all x1, blocking collectives, body(): lax.all_to_all(iface_adj, 'se', split_axis=1, concat_axis=0, tiled=True)  22.8 us
    gather x1, local copies, waits for them, and re-layouts, body(): jnp.take(fn_piece.reshape(how_many, -1, NB), connectivity, axis=1)  11.2 us
    unnamed x8, local copies, waits for them, and re-layouts  8.16 us
  transfers between devices with their start and end apart: 2, of which 1 were waited for; matrix products, arithmetic and copies ran while one was open for 20% of the time, Pallas kernels for 0%

commit v1 on v0

v1 whole, which is shorter than its diff:
```python
import jax
import jax.numpy as jnp
from jax import lax
from jax.experimental import pallas as pl
from jax.experimental.pallas import tpu as pltpu
from jax.sharding import PartitionSpec as P

NB = 96
NBLK = 16
NV = 2048
FN = 4
SEA = 32
ROWS = 96
COLS = 3072
FUNCS = FN * ROWS
M = NBLK * NB
LANES = 128
BF16 = jnp.bfloat16
F32 = jnp.float32
MESH = pl.DeviceIdType.MESH
NT = (((1,), (1,)), ((), ()))


def greet(se_peers, fn_peers):
    me, z = lax.axis_index("se"), lax.axis_index("fn")
    barrier = pltpu.get_barrier_semaphore()

    @pl.loop(1, SEA)
    def _(o):
        pl.semaphore_signal(barrier, inc=1, device_id={"se": lax.rem(me + o, SEA)}, device_id_type=MESH)

    for o in fn_peers:
        pl.semaphore_signal(barrier, inc=1, device_id={"fn": lax.rem(z + o, FN)}, device_id_type=MESH)
    pl.semaphore_wait(barrier, SEA - 1 + len(fn_peers))


def gather_kernel(x, out, recv, wide, own, send1, recv1, zsend, zrecv, lsem):
    me, z = lax.axis_index("se"), lax.axis_index("fn")
    greet(SEA, (1, 3))

    def piece(target, source):
        return pltpu.make_async_remote_copy(
            src_ref=x.at[:, pl.ds(pl.multiple_of(target * COLS, COLS), COLS)],
            dst_ref=recv.at[source],
            send_sem=send1.at[target],
            recv_sem=recv1.at[source],
            device_id={"se": target},
            device_id_type=MESH,
        )

    @pl.loop(1, SEA)
    def _(o):
        piece(lax.rem(me + o, SEA), me).start()

    mine = pltpu.make_async_copy(x.at[:, pl.ds(pl.multiple_of(me * COLS, COLS), COLS)], recv.at[me], lsem)
    mine.start()
    mine.wait()

    @pl.loop(1, SEA)
    def _(o):
        source = lax.rem(me + SEA - o, SEA)
        piece(source, source).wait_recv()

    @pl.loop(0, SEA // 8)
    def _(g):
        for u in range(8):
            wide[g, 3 * u : 3 * u + 3, :] = recv[g * 8 + u].astype(F32)

    own[...] = wide[...].reshape(ROWS, COLS).astype(BF16)

    right, left, far = lax.rem(z + 1, FN), lax.rem(z + 3, FN), lax.rem(z + 2, FN)
    half = ROWS // 2

    def slot(owner, h):
        return out.at[pl.ds(pl.multiple_of(owner * ROWS + h * half, half), half), :]

    def send(src, owner, h, target, n):
        return pltpu.make_async_remote_copy(
            src_ref=src,
            dst_ref=slot(owner, h),
            send_sem=zsend.at[n],
            recv_sem=zrecv.at[n],
            device_id={"fn": target},
            device_id_type=MESH,
        )

    def own_half(h):
        return own.at[pl.ds(h * half, half), :]

    r0, r1 = send(own_half(0), z, 0, right, 0), send(own_half(1), z, 1, right, 1)
    l1, l0 = send(own_half(1), z, 1, left, 2), send(own_half(0), z, 0, left, 3)
    r0.start()
    l1.start()
    r1.start()
    l0.start()
    keep = pltpu.make_async_copy(own, out.at[pl.ds(pl.multiple_of(z * ROWS, ROWS), ROWS), :], lsem)
    keep.start()
    r0.wait_recv()
    rr = send(slot(left, 0), left, 0, right, 4)
    rr.start()
    l1.wait_recv()
    ll = send(slot(right, 1), right, 1, left, 5)
    ll.start()
    keep.wait()
    for c in (r1, l0, rr, ll):
        c.wait_recv()
    for c in (r0, r1, l0, l1, rr, ll):
        c.wait_send()

    @pl.loop(1, SEA)
    def _(o):
        piece(lax.rem(me + o, SEA), me).wait_send()


def gather(x):
    return pl.pallas_call(
        gather_kernel,
        out_shape=jax.ShapeDtypeStruct((FUNCS, COLS), BF16),
        in_specs=[pl.BlockSpec(memory_space=pl.ANY)],
        out_specs=pl.BlockSpec(memory_space=pl.ANY),
        scratch_shapes=[
            pltpu.VMEM((SEA, 3, COLS), BF16),
            pltpu.VMEM((SEA // 8, 24, COLS), F32),
            pltpu.VMEM((ROWS, COLS), BF16),
            pltpu.SemaphoreType.DMA((SEA,)),
            pltpu.SemaphoreType.DMA((SEA,)),
            pltpu.SemaphoreType.DMA((6,)),
            pltpu.SemaphoreType.DMA((6,)),
            pltpu.SemaphoreType.DMA,
        ],
        compiler_params=pltpu.CompilerParams(collective_id=0, has_side_effects=True, vmem_limit_bytes=24 << 20),
    )(x)


def panel_kernel(conn, piece, panel, mask, terms, out, sums, rot, expand, bound, masked):
    s = pl.program_id(0)

    @pl.when(s == 0)
    def _():
        sums[...] = jnp.zeros_like(sums)
        block = lax.broadcasted_iota(jnp.int32, (NBLK, M), 1) // NB
        row = lax.broadcasted_iota(jnp.int32, (NBLK, M), 0)
        expand[...] = jnp.where(block == row, -1.0, 0.0).astype(BF16)

        @pl.loop(0, COLS // (4 * NB))
        def _(g):
            cols = piece[:, pl.ds(pl.multiple_of(g * 4 * NB, 4 * NB), 4 * NB)].astype(F32)
            for u in range(4):
                part = cols[:, u * NB : (u + 1) * NB]
                first = jnp.concatenate([part, jnp.zeros((FUNCS, LANES - NB), F32)], axis=1)
                rot[0, g * 4 + u] = first.astype(BF16)
                for r in range(1, 4):
                    rot[r, g * 4 + u] = pltpu.roll(first, LANES - 32 * r, 1).astype(BF16)

    keep = jnp.dot(mask[s].astype(F32).astype(BF16), expand[...], preferred_element_type=F32).astype(BF16)
    for i in range(4):
        masked[i * NB : (i + 1) * NB, :] = panel[0, i * NB : (i + 1) * NB, :] * keep[i : i + 1, :]

    lane = lax.broadcasted_iota(jnp.int32, (FUNCS, LANES), 1)
    for g in range(4):
        a, b, c, d = (rot.at[u, conn[s, 4 * g + u]] for u in range(4))
        at = g * 4 * NB
        b_, c_ = b[...], c[...]
        bound[:, at : at + LANES] = jnp.where(lane < 96, a[...], b_)
        bound[:, at + LANES : at + 2 * LANES] = jnp.where(lane < 64, b_, c_)
        bound[:, at + 2 * LANES : at + 3 * LANES] = jnp.where(lane < 32, c_, d[...])

    interior = lax.dot_general(bound[...], masked[...], NT, preferred_element_type=F32)
    high = interior.astype(BF16)
    out[0] = high
    low = (interior - high.astype(F32)).astype(BF16)

    w = terms[pl.ds(s, 1), :]
    w_high = w.astype(BF16).astype(F32)
    row = lax.broadcasted_iota(jnp.int32, (LANES, 4 * NB), 0)
    block = lax.broadcasted_iota(jnp.int32, (LANES, 4 * NB), 1) // NB
    held = jnp.where(row < 64, w_high, w - w_high)
    held = jnp.where((row & 63) == 4 * s + block, held, 0.0).astype(BF16)
    sums[...] += lax.dot_general(
        jnp.concatenate([high, low], axis=1), jnp.concatenate([held, held], axis=1), NT, preferred_element_type=F32
    )

    @pl.when(s == pl.num_programs(0) - 1)
    def _():
        total = sums[...]
        sums[...] = total + pltpu.roll(total, 64, 1)


def panels_step(piece, panels, block_mask, connectivity, state_terms):
    count = panels.shape[0]
    rows = panels.shape[1]
    return pl.pallas_call(
        panel_kernel,
        out_shape=(
            jax.ShapeDtypeStruct((count, FUNCS, rows), BF16),
            jax.ShapeDtypeStruct((FUNCS, LANES), F32),
        ),
        grid_spec=pltpu.PrefetchScalarGridSpec(
            num_scalar_prefetch=1,
            grid=(count,),
            in_specs=[
                pl.BlockSpec((FUNCS, COLS), lambda s, c: (0, 0)),
                pl.BlockSpec((1, rows, M), lambda s, c: (s, 0, 0)),
                pl.BlockSpec((count, 4, NBLK), lambda s, c: (0, 0, 0)),
                pl.BlockSpec((count, rows), lambda s, c: (0, 0)),
            ],
            out_specs=(
                pl.BlockSpec((1, FUNCS, rows), lambda s, c: (s, 0, 0)),
                pl.BlockSpec((FUNCS, LANES), lambda s, c: (0, 0)),
            ),
            scratch_shapes=[
                pltpu.VMEM((4, COLS // NB, FUNCS, LANES), BF16),
                pltpu.VMEM((NBLK, M), BF16),
                pltpu.VMEM((FUNCS, M), BF16),
                pltpu.VMEM((rows, M), BF16),
            ],
        ),
        compiler_params=pltpu.CompilerParams(vmem_limit_bytes=48 << 20),
        cost_estimate=pl.CostEstimate(flops=7_250_000_000, bytes_accessed=27_000_000, transcendentals=0),
    )(connectivity, piece, panels, block_mask, state_terms)


def gradient_kernel(sums, var, out, msg, mid, got, zsend, zrecv, send2, recv2):
    me, z = lax.axis_index("se"), lax.axis_index("fn")
    low_lane = lax.broadcasted_iota(jnp.int32, (LANES, LANES), 1) < 64
    parts = [sums[pl.ds(a, LANES, stride=3), :] for a in range(3)]
    msg[:, 0, :] = jnp.where(low_lane, parts[0], parts[1])
    msg[:, 1, :] = jnp.where(low_lane, parts[2], var[...])
    greet(SEA, (1, 2, 3))

    def along(target, source, n):
        return pltpu.make_async_remote_copy(
            src_ref=msg.at[pl.ds(target * SEA, SEA)],
            dst_ref=mid.at[source],
            send_sem=zsend.at[n],
            recv_sem=zrecv.at[n],
            device_id={"fn": target},
            device_id_type=MESH,
        )

    for o in range(1, FN):
        along(lax.rem(z + o, FN), z, o).start()
    mid[z] = msg[pl.ds(z * SEA, SEA)]
    for o in range(1, FN):
        source = lax.rem(z + FN - o, FN)
        along(source, source, o).wait_recv()

    def across(target, source):
        return pltpu.make_async_remote_copy(
            src_ref=mid.at[:, target],
            dst_ref=got.at[pl.ds(source * FN, FN)],
            send_sem=send2.at[target],
            recv_sem=recv2.at[source],
            device_id={"se": target},
            device_id_type=MESH,
        )

    @pl.loop(1, SEA)
    def _(o):
        across(lax.rem(me + o, SEA), me).start()

    got[pl.ds(me * FN, FN)] = mid[:, me]

    @pl.loop(1, SEA)
    def _(o):
        source = lax.rem(me + SEA - o, SEA)
        across(source, source).wait_recv()

    first, second = got[:, 0, :].T, got[:, 1, :].T
    x = [first[:64], first[64:], second[:64]]
    v = second[64:]
    v_high = jnp.floor(v * (1.0 / 128.0))
    v_low = v - 128.0 * v_high
    group = lax.broadcasted_iota(jnp.int32, (16, 2 * LANES), 0).astype(F32)
    place = lax.broadcasted_iota(jnp.int32, (LANES, 2 * LANES), 0).astype(F32)

    def pair(t, q):
        return jnp.concatenate([t[2 * q : 2 * q + 1], t[2 * q + 1 : 2 * q + 2]], axis=1)

    total = jnp.zeros((96, LANES), F32)
    for q in range(32):
        in_group = group == pair(v_high, q)
        rows = []
        for a in range(3):
            value = pair(x[a], q)
            high = value.astype(BF16).astype(F32)
            rows.append(jnp.where(in_group, high, 0.0).astype(BF16))
            rows.append(jnp.where(in_group, value - high, 0.0).astype(BF16))
        here = jnp.where(place == pair(v_low, q), 1.0, 0.0).astype(BF16)
        total += lax.dot_general(jnp.concatenate(rows, axis=0), here, NT, preferred_element_type=F32)
    for a in range(3):
        out[a] = total[32 * a : 32 * a + 16] + total[32 * a + 16 : 32 * a + 32]

    for o in range(1, FN):
        along(lax.rem(z + o, FN), z, o).wait_send()

    @pl.loop(1, SEA)
    def _(o):
        across(lax.rem(me + o, SEA), me).wait_send()


def gradient(sums, var):
    return pl.pallas_call(
        gradient_kernel,
        out_shape=jax.ShapeDtypeStruct((3, NV // LANES, LANES), F32),
        in_specs=[pl.BlockSpec(memory_space=pltpu.VMEM)] * 2,
        out_specs=pl.BlockSpec(memory_space=pltpu.VMEM),
        scratch_shapes=[
            pltpu.VMEM((FN * SEA, 2, LANES), F32),
            pltpu.VMEM((FN, SEA, 2, LANES), F32),
            pltpu.VMEM((FN * SEA, 2, LANES), F32),
            pltpu.SemaphoreType.DMA((FN,)),
            pltpu.SemaphoreType.DMA((FN,)),
            pltpu.SemaphoreType.DMA((SEA,)),
            pltpu.SemaphoreType.DMA((SEA,)),
        ],
        compiler_params=pltpu.CompilerParams(collective_id=1, has_side_effects=True, vmem_limit_bytes=24 << 20),
    )(sums, var)


def body(iface_adj, panels, block_mask, connectivity, var_map, state_terms):
    piece = gather(iface_adj)
    interior, sums = panels_step(piece, panels, block_mask, connectivity, state_terms)
    var = var_map.astype(F32).reshape(1, 64)
    var = jnp.concatenate([var, var], axis=1)
    grad = gradient(sums, var)
    return interior, grad.reshape(3, NV)


def solution(mesh):
    placed = (
        P(("fn", "se"), None),
        P("se", "fn", None),
        P("se", "fn", None),
        P("se", None),
        P("se", "fn"),
        P("se", "fn"),
    )
    return jax.shard_map(
        body,
        mesh=mesh,
        in_specs=placed,
        out_specs=(P("se", None, "fn"), P(("fn", "se"), None)),
        check_vma=False,
    )
```

time: 292 us -> 93 us (0.32)
  waiting for transfers between devices: 145 us -> 0 us
  Pallas kernels: 0 us -> 87.4 us
  local copies, waits for them, and re-layouts: 74.1 us -> 4.12 us
  matrix products: 28.1 us -> 0 us
  blocking collectives: 22.8 us -> 0 us
  between operations: 14.1 us -> 0.67 us
  other arithmetic: 5.89 us -> 0.08 us
    unnamed x3 -> x0, waiting for transfers between devices: 145 us -> none
    pallas_call x0 -> x3, Pallas kernels: none -> 87.4 us  [the longest x1 41.9 us: gather(): pl.pallas_call(gather_kernel, out_shape=jax.ShapeDtypeStruct((FUNCS, COLS...]
    mul x3 -> x0, local copies, waits for them, and re-layouts: 50.1 us -> none  [the longest x2 50.1 us: body(): panels.reshape(local_count, row_blocks, NB, NBLK, NB)]
    dot_general x2 -> x0, matrix products: 28.1 us -> none  [the longest x1 25 us: body(): jnp.einsum('fsm,srm->sfr', boundary, blocks, preferred_element_type=jnp.f...]
    all_to_all x1 -> x0, blocking collectives: 22.8 us -> none  [body(): lax.all_to_all(iface_adj, 'se', split_axis=1, concat_axis=0, tiled=True)]
    gather x1 -> x0, local copies, waits for them, and re-layouts: 11.2 us -> none  [body(): jnp.take(fn_piece.reshape(how_many, -1, NB), connectivity, axis=1)]
    reduce_sum x1 -> x0, other arithmetic: 5.1 us -> none  [body(): jnp.sum(interior.reshape(local_count, func_count, row_blocks, NB) * weigh...]
    unnamed x8 -> x11, local copies, waits for them, and re-layouts: 8.16 us -> 3.95 us
  transfers between devices with their start and end apart: 2 -> 0, of which waited for: 1 -> 0; matrix products, arithmetic and copies ran while one was open for 20% -> 0% of each run, Pallas kernels for 0% -> 0%
where the time goes in v1:
time: 93 us; the launch traced here: 92.2 us
  Pallas kernels  87.4 us (94%)
  local copies, waits for them, and re-layouts  4.12 us (4%)
    pallas_call x1, Pallas kernels, gather(): pl.pallas_call(gather_kernel, out_shape=jax.ShapeDtypeStruct((FUNCS, COLS...  41.9 us
    pallas_call x1, Pallas kernels, panels_step(): pl.pallas_call(panel_kernel, out_shape=(jax.ShapeDtypeStruct((count, FUNC...  28.3 us
    pallas_call x1, Pallas kernels, gradient(): pl.pallas_call(gradient_kernel, out_shape=jax.ShapeDtypeStruct((3, NV //...  17.2 us
    unnamed x11, local copies, waits for them, and re-layouts  3.95 us

profile of v1, /device:TPU:1, one launch (start us, length us, event | category | flops | bytes accessed | tf_op | source)
XLA Modules:
  0.0 92.2 jit_solution(2707250028363468099)
XLA Ops:
  0.6 0.0 copy-start
  0.6 1.1 %copy-done = bf16[3,98304]{1,0:T(4,128)(2,1)S(1)} copy-done((bf16[3,98304]{1,0:T(4,128)(2,1)S(1)}, bf16[3,98304]{1,0:T(4,128)(2,1)}, u32[]{:S(2)}) %copy-start) | copy-done | bytes 589848
  1.8 41.9 %shard_map.77.piece = bf16[384,3072]{1,0:T(8,128)(2,1)S(1)} custom-call(bf16[3,98304]{1,0:T(4,128)(2,1)S(1)} %copy-done), custom_call_target="tpu_custom_call" | custom-call | tf_op jit(solution)/shard_map/pallas_call | solution.py:116
  43.6 0.0 copy-start.1
  43.6 0.7 copy-done.1
  44.4 0.0 copy-start.2
  44.4 0.7 copy-done.2
  45.1 0.0 copy-start.3
  45.1 0.7 copy-done.3
  45.8 0.0 copy-start.4
  45.8 28.3 %shard_map.78 = (bf16[16,384,384]{2,1,0:T(8,128)(2,1)}, f32[384,128]{1,0:T(8,128)S(1)}) custom-call(s32[16,16]{1,0:T(8,128)S(1)} %copy-done.3, bf16[384,3072]{1,0:T(8,128)(2,1)S(1)} %shard_map.77.piece, bf16[16,384,1536]{2,1,0:T(8,128)(2,1)} %panel.1, s32[16,4,16]{2,1,0:T(4,128)S(1)} %copy-done.1, f32[16,384]{1,0:T(8,128)S(1)} %copy-done.2), custom_call_target="tpu_custom_call" | custom-call | flops 7249999872 | bytes 27000000 | tf_op jit(solution)/shard_map/pallas_call | solution.py:192
  74.1 0.0 copy-done.4
  74.1 0.1 copy.9
  74.2 0.1 reshape.10
  74.3 0.1 pad_maximum_fusion.var
  74.4 17.2 %shard_map.79 = f32[3,16,128]{2,1,0:T(8,128)S(1)} custom-call(f32[384,128]{1,0:T(8,128)S(1)} %get-tuple-element.5.sums, f32[1,128]{1,0:T(1,128)S(1)} %pad_maximum_fusion.var), custom_call_target="tpu_custom_call" | custom-call | tf_op jit(solution)/shard_map/pallas_call | solution.py:303
  91.6 0.6 copy.12
  (1 shorter events, 0.0 us)
Async XLA Ops:
  0.6 1.1 %copy-start = (bf16[3,98304]{1,0:T(4,128)(2,1)S(1)}, bf16[3,98304]{1,0:T(4,128)(2,1)}, u32[]{:S(2)}) copy-start(bf16[3,98304]{1,0:T(4,128)(2,1)} %x.1) | copy-start | bytes 1769476
  43.6 0.8 copy-start.1
  44.4 0.7 copy-start.2
  45.1 0.7 copy-start.3
  45.8 28.3 %copy-start.4 = (s32[16,4]{0,1:T(4,128)S(1)}, s32[16,4]{0,1:T(4,128)}, u32[]{:S(2)}) copy-start(s32[16,4]{0,1:T(4,128)} %param.10) | copy-start | bytes 772

commit v2 on v0

v2 whole, which is shorter than its diff:
```python
import jax
import jax.numpy as jnp
from jax import lax
from jax.experimental import pallas as pl
from jax.experimental.pallas import tpu as pltpu
from jax.sharding import PartitionSpec as P

NB = 96
NBLK = 16
NV = 2048
FN = 4
SEA = 32
ROWS = 96
COLS = 3072
FUNCS = FN * ROWS
M = NBLK * NB
LANES = 128
BF16 = jnp.bfloat16
F32 = jnp.float32
MESH = pl.DeviceIdType.MESH
NT = (((1,), (1,)), ((), ()))
WIDE = 512
LIMIT_A = 12
LIMIT_B = 12
CHUNKS = 4
PART = COLS // CHUNKS
HALF = ROWS // 2


def gather_kernel(
    x, panels, mask_in, terms_in, pext, rot, recv, wide, planes, mask, terms, expand,
    small, psem, send1, recv1, zsend, zrecv,
):
    me, z = lax.axis_index("se"), lax.axis_index("fn")
    right, left, far = lax.rem(z + 1, FN), lax.rem(z + 3, FN), lax.rem(z + 2, FN)
    count = panels.shape[0]

    barrier = pltpu.get_barrier_semaphore()

    @pl.loop(1, SEA)
    def _(o):
        pl.semaphore_signal(barrier, inc=1, device_id={"se": lax.rem(me + o, SEA)}, device_id_type=MESH)

    for t in (right, left):
        pl.semaphore_signal(barrier, inc=1, device_id={"fn": t}, device_id_type=MESH)

    def columns(target, q):
        return x.at[:, pl.ds(pl.multiple_of(target * COLS + q * PART, PART), PART)]

    smalls = [
        pltpu.make_async_copy(a, b, small.at[n]) for n, (a, b) in enumerate(((mask_in, mask), (terms_in, terms)))
    ]
    mine = [pltpu.make_async_copy(columns(me, q), recv.at[q, me], small.at[2 + q]) for q in range(CHUNKS)]
    for c in (*smalls, *mine):
        c.start()

    def panel(s):
        return pltpu.make_async_copy(panels.at[s], pext.at[s, pl.ds(0, 4 * NB), :], psem.at[s])

    @pl.loop(0, count)
    def _(s):
        panel(s).start()

    pl.semaphore_wait(barrier, SEA - 1 + 2)

    def piece(target, source, q):
        return pltpu.make_async_remote_copy(
            src_ref=columns(target, q),
            dst_ref=recv.at[q, source],
            send_sem=send1.at[q, target],
            recv_sem=recv1.at[q, source],
            device_id={"se": target},
            device_id_type=MESH,
        )

    for q in range(CHUNKS):

        @pl.loop(1, SEA)
        def _(o):
            piece(lax.rem(me + o, SEA), me, q).start()

    for c in smalls:
        c.wait()
    block = lax.broadcasted_iota(jnp.int32, (NBLK, M), 1) // NB
    row = lax.broadcasted_iota(jnp.int32, (NBLK, M), 0)
    expand[...] = jnp.where(block == row, -1.0, 0.0).astype(BF16)

    def prepare(s):
        panel(s).wait()
        keep = jnp.dot(mask[s].astype(F32).astype(BF16), expand[...], preferred_element_type=F32).astype(BF16)
        for i in range(4):
            rows = pl.ds(i * NB, NB)
            pext[s, rows, :] = pext[s, rows, :] * keep[i : i + 1, :]
        w = terms[pl.ds(s, 1), :]
        w_high = w.astype(BF16).astype(F32)
        at = lax.broadcasted_iota(jnp.int32, (LANES, 4 * NB), 0)
        of = lax.broadcasted_iota(jnp.int32, (LANES, 4 * NB), 1) // NB
        held = jnp.where(at < 64, w_high, w - w_high)
        held = jnp.where((at & 63) == 4 * s + of, held, 0.0).astype(BF16)
        both = jnp.dot(held, pext[s, pl.ds(0, 4 * NB), :], preferred_element_type=F32)
        total = both[:64] + both[64:]
        high = total.astype(BF16)
        pext[s, pl.ds(4 * NB, 64), :] = high
        pext[s, pl.ds(4 * NB + 64, 64), :] = (total - high.astype(F32)).astype(BF16)

    def pack(q):
        mine[q].wait()

        @pl.loop(1, SEA)
        def _(o):
            source = lax.rem(me + SEA - o, SEA)
            piece(source, source, q).wait_recv()

        @pl.loop(0, SEA // 8)
        def _(g):
            for u in range(8):
                wide[g, 3 * u : 3 * u + 3, :] = recv[q, g * 8 + u].astype(F32)

        planes[q, z] = wide[...].reshape(ROWS, PART).astype(BF16)

    def send(owner, h, target, n, q):
        part = planes.at[q, owner, pl.ds(h * HALF, HALF), :]
        return pltpu.make_async_remote_copy(
            src_ref=part,
            dst_ref=part,
            send_sem=zsend.at[6 * q + n],
            recv_sem=zrecv.at[6 * q + n],
            device_id={"fn": target},
            device_id_type=MESH,
        )

    def sends(q):
        return [send(z, 0, right, 0, q), send(z, 1, left, 2, q), send(z, 1, right, 1, q), send(z, 0, left, 3, q)]

    def onward(q):
        return send(left, 0, right, 4, q)

    def backward(q):
        return send(right, 1, left, 5, q)

    def relay(q):
        send(left, 0, right, 0, q).wait_recv()
        onward(q).start()
        send(right, 1, left, 2, q).wait_recv()
        backward(q).start()

    def rotate(owner, q):
        @pl.loop(0, PART // (4 * NB))
        def _(g):
            cols = planes[q, owner, :, pl.ds(pl.multiple_of(g * 4 * NB, 4 * NB), 4 * NB)].astype(F32)
            rows = pl.ds(pl.multiple_of(owner * ROWS, ROWS), ROWS)
            for u in range(4):
                part = cols[:, u * NB : (u + 1) * NB]
                first = jnp.concatenate([part, jnp.zeros((ROWS, LANES - NB), F32)], axis=1)
                for r in range(4):
                    turned = first if r == 0 else pltpu.roll(first, LANES - 32 * r, 1)
                    rot[r, q * (PART // NB) + g * 4 + u, rows, :] = turned.astype(BF16)

    for q in range(CHUNKS):
        pl.loop(q * (count // CHUNKS), (q + 1) * (count // CHUNKS))(prepare)
        pack(q)
        for c in sends(q):
            c.start()
        if q:
            relay(q - 1)
        rotate(z, q)
    relay(CHUNKS - 1)
    for q in range(CHUNKS):
        send(left, 1, right, 1, q).wait_recv()
        rotate(left, q)
        send(right, 0, left, 3, q).wait_recv()
        rotate(right, q)
    for q in range(CHUNKS):
        send(far, 0, right, 4, q).wait_recv()
        send(far, 1, left, 5, q).wait_recv()
        rotate(far, q)
    for q in range(CHUNKS):
        for c in (*sends(q), onward(q), backward(q)):
            c.wait_send()

        @pl.loop(1, SEA)
        def _(o):
            piece(lax.rem(me + o, SEA), me, q).wait_send()


def panel_kernel(rot, pext, conn, out, sums, stage, osem):
    lane = lax.broadcasted_iota(jnp.int32, (FUNCS, LANES), 1)
    count = out.shape[0]

    def store(s, k):
        return pltpu.make_async_copy(stage.at[k], out.at[s], osem.at[k])

    sums[...] = jnp.zeros_like(sums)

    @pl.loop(0, count // 2)
    def _(pair):
        for k in range(2):
            s = 2 * pair + k
            tiles = []
            for g in range(4):
                a, b, c, d = (rot[u, conn[s, 4 * g + u]] for u in range(4))
                tiles += [jnp.where(lane < 96, a, b), jnp.where(lane < 64, b, c), jnp.where(lane < 32, c, d)]
            bound = jnp.concatenate(tiles, axis=1)
            found = lax.dot_general(bound, pext[s], NT, preferred_element_type=F32)

            @pl.when(pair > 0)
            def _():
                store(s, k).wait()

            stage[k] = found[:, : 4 * NB].astype(BF16)
            store(s, k).start()
            sums[...] += found[:, 4 * NB :]

    for k in range(2):
        store(k, k).wait()
    total = sums[...]
    sums[...] = total + pltpu.roll(total, 64, 1)


def gradient_kernel(sums, var, out, msg, mid, turned, got, zsend, zrecv, send2, recv2):
    me, z = lax.axis_index("se"), lax.axis_index("fn")
    barrier = pltpu.get_barrier_semaphore()

    @pl.loop(1, SEA)
    def _(o):
        pl.semaphore_signal(barrier, inc=1, device_id={"se": lax.rem(me + o, SEA)}, device_id_type=MESH)

    for o in range(1, FN):
        pl.semaphore_signal(barrier, inc=1, device_id={"fn": lax.rem(z + o, FN)}, device_id_type=MESH)

    v = var[...].astype(F32)
    v_high = jnp.floor(v * (1.0 / 128.0))
    v_low = v - 128.0 * v_high
    lane16 = lax.broadcasted_iota(jnp.int32, (NBLK, LANES), 1)
    row16 = lax.broadcasted_iota(jnp.int32, (NBLK, LANES), 0)
    spread = jnp.where((lane16 & 63) // 4 == row16, 1.0, 0.0).astype(BF16)
    ids = 128.0 * jnp.dot(v_high.astype(BF16), spread, preferred_element_type=F32) + jnp.dot(
        v_low.astype(BF16), spread, preferred_element_type=F32
    )
    lane4 = lax.broadcasted_iota(jnp.int32, (4, LANES), 1)
    row4 = lax.broadcasted_iota(jnp.int32, (4, LANES), 0)
    ids = jnp.sum(jnp.where((lane4 & 3) == row4, ids, 0.0), axis=0, keepdims=True)

    low_lane = lax.broadcasted_iota(jnp.int32, (SEA, LANES), 1) < 64
    for t in range(FN):
        parts = [sums[pl.ds(t * ROWS + a, SEA, stride=3), :] for a in range(3)]
        msg[t, pl.ds(0, SEA, stride=2), :] = jnp.where(low_lane, parts[0], parts[1])
        msg[t, pl.ds(1, SEA, stride=2), :] = jnp.where(low_lane, parts[2], ids)
    pl.semaphore_wait(barrier, SEA - 1 + 3)

    def along(target, source, n):
        return pltpu.make_async_remote_copy(
            src_ref=msg.at[target],
            dst_ref=mid.at[source],
            send_sem=zsend.at[n],
            recv_sem=zrecv.at[n],
            device_id={"fn": target},
            device_id_type=MESH,
        )

    for o in (2, 1, 3):
        along(lax.rem(z + o, FN), z, o).start()
    mid[z] = msg[z]
    for o in (1, 3, 2):
        along(z, lax.rem(z + FN - o, FN), o).wait_recv()
    for t in range(FN):
        for h in range(2):
            turned[pl.ds(2 * t + h, SEA, stride=8), :] = mid[t, pl.ds(h, SEA, stride=2), :]

    def across(target, source):
        return pltpu.make_async_remote_copy(
            src_ref=turned.at[pl.ds(pl.multiple_of(target * 8, 8), 8)],
            dst_ref=got.at[pl.ds(pl.multiple_of(source * 8, 8), 8)],
            send_sem=send2.at[target],
            recv_sem=recv2.at[source],
            device_id={"se": target},
            device_id_type=MESH,
        )

    @pl.loop(1, SEA)
    def _(o):
        across(lax.rem(me + o, SEA), me).start()

    own = pl.ds(pl.multiple_of(me * 8, 8), 8)
    got[own] = turned[own]

    @pl.loop(1, SEA)
    def _(o):
        source = lax.rem(me + SEA - o, SEA)
        across(source, source).wait_recv()

    first, second = got[pl.ds(0, LANES, stride=2), :].T, got[pl.ds(1, LANES, stride=2), :].T
    x = [first[:64], first[64:], second[:64]]
    v = second[64:]
    v_high = jnp.floor(v * (1.0 / 128.0))
    v_low = v - 128.0 * v_high
    group = lax.broadcasted_iota(jnp.int32, (16, 2 * LANES), 0).astype(F32)
    place = lax.broadcasted_iota(jnp.int32, (LANES, 2 * LANES), 0).astype(F32)

    def pair(t, q):
        return jnp.concatenate([t[2 * q : 2 * q + 1], t[2 * q + 1 : 2 * q + 2]], axis=1)

    total = jnp.zeros((96, LANES), F32)
    for q in range(32):
        in_group = group == pair(v_high, q)
        rows = []
        for a in range(3):
            value = pair(x[a], q)
            high = value.astype(BF16).astype(F32)
            rows.append(jnp.where(in_group, high, 0.0).astype(BF16))
            rows.append(jnp.where(in_group, value - high, 0.0).astype(BF16))
        here = jnp.where(place == pair(v_low, q), 1.0, 0.0).astype(BF16)
        total += lax.dot_general(jnp.concatenate(rows, axis=0), here, NT, preferred_element_type=F32)
    for a in range(3):
        out[a] = total[32 * a : 32 * a + 16] + total[32 * a + 16 : 32 * a + 32]

    for o in range(1, FN):
        along(lax.rem(z + o, FN), z, o).wait_send()

    @pl.loop(1, SEA)
    def _(o):
        across(lax.rem(me + o, SEA), me).wait_send()


def body(iface_adj, panels, block_mask, connectivity, var_map, state_terms):
    count, rows = panels.shape[0], panels.shape[1]
    hbm = pl.BlockSpec(memory_space=pltpu.HBM)
    vmem = pl.BlockSpec(memory_space=pltpu.VMEM)
    dma = pltpu.SemaphoreType.DMA
    far_operands = [pltpu.with_memory_space_constraint(a, pltpu.HBM) for a in (iface_adj, panels, block_mask, state_terms)]
    pext, rot = pl.pallas_call(
        gather_kernel,
        out_shape=(
            pltpu.VMEM((count, WIDE, M), BF16),
            pltpu.VMEM((4, COLS // NB, FUNCS, LANES), BF16),
        ),
        in_specs=[hbm] * 4,
        out_specs=(vmem, vmem),
        scratch_shapes=[
            pltpu.VMEM((CHUNKS, SEA, 3, PART), BF16),
            pltpu.VMEM((SEA // 8, 24, PART), F32),
            pltpu.VMEM((CHUNKS, FN, ROWS, PART), BF16),
            pltpu.VMEM(block_mask.shape, jnp.int32),
            pltpu.VMEM(state_terms.shape, F32),
            pltpu.VMEM((NBLK, M), BF16),
            dma((2 + CHUNKS,)),
            dma((count,)),
            dma((CHUNKS, SEA)),
            dma((CHUNKS, SEA)),
            dma((6 * CHUNKS,)),
            dma((6 * CHUNKS,)),
        ],
        compiler_params=pltpu.CompilerParams(collective_id=0, has_side_effects=True, vmem_limit_bytes=LIMIT_A << 20),
    )(*far_operands)
    interior, sums = pl.pallas_call(
        panel_kernel,
        out_shape=(
            jax.ShapeDtypeStruct((count, FUNCS, rows), BF16),
            pltpu.VMEM((FUNCS, LANES), F32),
        ),
        in_specs=[vmem, vmem, pl.BlockSpec(memory_space=pltpu.SMEM)],
        out_specs=(pl.BlockSpec(memory_space=pl.ANY), vmem),
        scratch_shapes=[pltpu.VMEM((2, FUNCS, rows), BF16), dma((2,))],
        compiler_params=pltpu.CompilerParams(vmem_limit_bytes=LIMIT_B << 20),
        cost_estimate=pl.CostEstimate(flops=9_700_000_000, bytes_accessed=5_000_000, transcendentals=0),
    )(rot, pext, connectivity)
    grad = pl.pallas_call(
        gradient_kernel,
        out_shape=jax.ShapeDtypeStruct((3, NV // LANES, LANES), F32),
        in_specs=[vmem, vmem],
        out_specs=vmem,
        scratch_shapes=[
            pltpu.VMEM((FN, 2 * SEA, LANES), F32),
            pltpu.VMEM((FN, 2 * SEA, LANES), F32),
            pltpu.VMEM((8 * SEA, LANES), F32),
            pltpu.VMEM((8 * SEA, LANES), F32),
            dma((FN,)),
            dma((FN,)),
            dma((SEA,)),
            dma((SEA,)),
        ],
        compiler_params=pltpu.CompilerParams(collective_id=1, has_side_effects=True, vmem_limit_bytes=8 << 20),
    )(sums, var_map.T)
    return interior, grad.reshape(3, NV)


def solution(mesh):
    placed = (
        P(("fn", "se"), None),
        P("se", "fn", None),
        P("se", "fn", None),
        P("se", None),
        P("se", "fn"),
        P("se", "fn"),
    )
    return jax.shard_map(
        body,
        mesh=mesh,
        in_specs=placed,
        out_specs=(P("se", None, "fn"), P(("fn", "se"), None)),
        check_vma=False,
    )
```

time: 292 us -> 75.7 us (0.26)
  waiting for transfers between devices: 145 us -> 0 us
  Pallas kernels: 0 us -> 74.3 us
  local copies, waits for them, and re-layouts: 74.1 us -> 0.64 us
  matrix products: 28.1 us -> 0 us
  blocking collectives: 22.8 us -> 0 us
  between operations: 14.1 us -> 0.69 us
  other arithmetic: 5.89 us -> 0 us
    unnamed x3 -> x0, waiting for transfers between devices: 145 us -> none
    pallas_call x0 -> x3, Pallas kernels: none -> 74.3 us  [the longest x1 44.8 us: body(): pl.pallas_call(gather_kernel, out_shape=(pltpu.VMEM((count, WIDE, M), BF1...]
    mul x3 -> x0, local copies, waits for them, and re-layouts: 50.1 us -> none  [the longest x2 50.1 us: body(): panels.reshape(local_count, row_blocks, NB, NBLK, NB)]
    dot_general x2 -> x0, matrix products: 28.1 us -> none  [the longest x1 25 us: body(): jnp.einsum('fsm,srm->sfr', boundary, blocks, preferred_element_type=jnp.f...]
    all_to_all x1 -> x0, blocking collectives: 22.8 us -> none  [body(): lax.all_to_all(iface_adj, 'se', split_axis=1, concat_axis=0, tiled=True)]
    gather x1 -> x0, local copies, waits for them, and re-layouts: 11.2 us -> none  [body(): jnp.take(fn_piece.reshape(how_many, -1, NB), connectivity, axis=1)]
    unnamed x8 -> x5, local copies, waits for them, and re-layouts: 8.16 us -> 0.64 us
    reduce_sum x1 -> x0, other arithmetic: 5.1 us -> none  [body(): jnp.sum(interior.reshape(local_count, func_count, row_blocks, NB) * weigh...]
  transfers between devices with their start and end apart: 2 -> 0, of which waited for: 1 -> 0; matrix products, arithmetic and copies ran while one was open for 20% -> 0% of each run, Pallas kernels for 0% -> 0%
where the time goes in v2:
time: 75.7 us; the launch traced here: 75.6 us
  Pallas kernels  74.3 us (98%)
    pallas_call x1, Pallas kernels, body(): pl.pallas_call(gather_kernel, out_shape=(pltpu.VMEM((count, WIDE, M), BF1...  44.8 us
    pallas_call x1, Pallas kernels, body(): pl.pallas_call(panel_kernel, out_shape=(jax.ShapeDtypeStruct((count, FUNC...  14.9 us
    pallas_call x1, Pallas kernels, body(): pl.pallas_call(gradient_kernel, out_shape=jax.ShapeDtypeStruct((3, NV //...  14.5 us

profile of v2, /device:TPU:1, one launch (start us, length us, event | category | flops | bytes accessed | tf_op | source)
XLA Modules:
  0.0 75.6 jit_solution(13720341279036850409)
XLA Ops:
  0.6 0.0 copy-start
  0.6 44.8 %shard_map.77 = (bf16[16,512,1536]{2,1,0:T(8,128)(2,1)S(1)}, bf16[4,32,384,128]{3,2,1,0:T(8,128)(2,1)S(1)}) custom-call(bf16[3,98304]{1,0:T(4,128)(2,1)} %x.1, bf16[16,384,1536]{2,1,0:T(8,128)(2,1)} %panels.1, s32[16,4,16]{2,1,0:T(4,128)} %mask_in.1, f32[16,384]{1,0:T(8,128)} %terms_in.1), custom_call_target="tpu_custom_call" | custom-call | tf_op jit(solution)/shard_map/pallas_call | solution.py:331
  45.5 0.0 copy-done
  45.5 0.0 copy-start.1
  45.5 14.9 %shard_map.78 = (bf16[16,384,384]{2,1,0:T(8,128)(2,1)}, f32[384,128]{1,0:T(8,128)S(1)}) custom-call(bf16[4,32,384,128]{3,2,1,0:T(8,128)(2,1)S(1)} %get-tuple-element.6.rot, bf16[16,512,1536]{2,1,0:T(8,128)(2,1)S(1)} %get-tuple-element.7.pext, s32[16,16]{1,0:T(8,128)S(1)} %copy-done), custom_call_target="tpu_custom_call" | custom-call | flops 9699999744 | bytes 5000000 | tf_op jit(solution)/shard_map/pallas_call | solution.py:355
  60.4 0.0 copy-done.1
  60.4 14.5 %shard_map.79 = f32[3,16,128]{2,1,0:T(8,128)S(1)} custom-call(f32[384,128]{1,0:T(8,128)S(1)} %get-tuple-element.9.sums, s32[4,16]{1,0:T(4,128)S(1)} %bitcast.6), custom_call_target="tpu_custom_call" | custom-call | tf_op jit(solution)/shard_map/pallas_call | solution.py:367
  75.0 0.6 copy.10
Async XLA Ops:
  0.6 44.8 %copy-start = (s32[16,16]{1,0:T(8,128)S(1)}, s32[16,16]{1,0:T(8,128)}, u32[]{:S(2)}) copy-start(s32[16,16]{1,0:T(8,128)} %conn.1) | copy-start | bytes 3076
  45.5 15.0 %copy-start.1 = (s32[16,4]{0,1:T(4,128)S(1)}, s32[16,4]{0,1:T(4,128)}, u32[]{:S(2)}) copy-start(s32[16,4]{0,1:T(4,128)} %param.10) | copy-start | bytes 772

commit v3 on v2

--- a/solution.py
+++ b/solution.py
@@ -22,7 +22,10 @@
 WIDE = 512
 LIMIT_A = 12
 LIMIT_B = 12
-CHUNKS = 4
+CHUNKS = 2
+EARLY = 4
+APART = 6
+UNROLL = 4
 PART = COLS // CHUNKS
 HALF = ROWS // 2
 
@@ -60,8 +63,6 @@
     @pl.loop(0, count)
     def _(s):
         panel(s).start()
-
-    pl.semaphore_wait(barrier, SEA - 1 + 2)
 
     def piece(target, source, q):
         return pltpu.make_async_remote_copy(
@@ -73,8 +74,7 @@
             device_id_type=MESH,
         )
 
-    for q in range(CHUNKS):
-
+    def issue(q):
         @pl.loop(1, SEA)
         def _(o):
             piece(lax.rem(me + o, SEA), me, q).start()
@@ -103,6 +103,13 @@
         pext[s, pl.ds(4 * NB, 64), :] = high
         pext[s, pl.ds(4 * NB + 64, 64), :] = (total - high.astype(F32)).astype(BF16)
 
+    pl.loop(0, EARLY)(prepare)
+    pl.semaphore_wait(barrier, SEA - 1 + 2)
+    for q in range(CHUNKS):
+        issue(q)
+        pl.loop(EARLY + q * APART, EARLY + (q + 1) * APART)(prepare)
+    done = EARLY + CHUNKS * APART
+
     def pack(q):
         mine[q].wait()
 
@@ -157,15 +164,21 @@
                     rot[r, q * (PART // NB) + g * 4 + u, rows, :] = turned.astype(BF16)
 
     for q in range(CHUNKS):
-        pl.loop(q * (count // CHUNKS), (q + 1) * (count // CHUNKS))(prepare)
         pack(q)
         for c in sends(q):
             c.start()
+        if q == 0:
+            pl.loop(done, count)(prepare)
         if q:
             relay(q - 1)
         rotate(z, q)
     relay(CHUNKS - 1)
     for q in range(CHUNKS):
+
+        @pl.loop(1, SEA)
+        def _(o):
+            piece(lax.rem(me + o, SEA), me, q).wait_send()
+    for q in range(CHUNKS):
         send(left, 1, right, 1, q).wait_recv()
         rotate(left, q)
         send(right, 0, left, 3, q).wait_recv()
@@ -178,10 +191,6 @@
         for c in (*sends(q), onward(q), backward(q)):
             c.wait_send()
 
-        @pl.loop(1, SEA)
-        def _(o):
-            piece(lax.rem(me + o, SEA), me, q).wait_send()
-
 
 def panel_kernel(rot, pext, conn, out, sums, stage, osem):
     lane = lax.broadcasted_iota(jnp.int32, (FUNCS, LANES), 1)
@@ -192,10 +201,10 @@
 
     sums[...] = jnp.zeros_like(sums)
 
-    @pl.loop(0, count // 2)
-    def _(pair):
-        for k in range(2):
-            s = 2 * pair + k
+    @pl.loop(0, count // UNROLL)
+    def _(turn):
+        for k in range(UNROLL):
+            s = UNROLL * turn + k
             tiles = []
             for g in range(4):
                 a, b, c, d = (rot[u, conn[s, 4 * g + u]] for u in range(4))
@@ -203,7 +212,7 @@
             bound = jnp.concatenate(tiles, axis=1)
             found = lax.dot_general(bound, pext[s], NT, preferred_element_type=F32)
 
-            @pl.when(pair > 0)
+            @pl.when(turn > 0)
             def _():
                 store(s, k).wait()
 
@@ -211,7 +220,7 @@
             store(s, k).start()
             sums[...] += found[:, 4 * NB :]
 
-    for k in range(2):
+    for k in range(UNROLL):
         store(k, k).wait()
     total = sums[...]
     sums[...] = total + pltpu.roll(total, 64, 1)
@@ -360,7 +369,7 @@
         ),
         in_specs=[vmem, vmem, pl.BlockSpec(memory_space=pltpu.SMEM)],
         out_specs=(pl.BlockSpec(memory_space=pl.ANY), vmem),
-        scratch_shapes=[pltpu.VMEM((2, FUNCS, rows), BF16), dma((2,))],
+        scratch_shapes=[pltpu.VMEM((UNROLL, FUNCS, rows), BF16), dma((UNROLL,))],
         compiler_params=pltpu.CompilerParams(vmem_limit_bytes=LIMIT_B << 20),
         cost_estimate=pl.CostEstimate(flops=9_700_000_000, bytes_accessed=5_000_000, transcendentals=0),
     )(rot, pext, connectivity)

time: 75.7 us -> 74.7 us (0.987)
  Pallas kernels: 74.3 us -> 73.3 us
    pallas_call x1, Pallas kernels: 44.8 us -> 41.6 us  [body(): pl.pallas_call(gather_kernel, out_shape=(pltpu.VMEM((count, WIDE, M), BF1...]
    pallas_call x1, Pallas kernels: 14.5 us -> 16.8 us  [body(): pl.pallas_call(gradient_kernel, out_shape=jax.ShapeDtypeStruct((3, NV //...]
where the time goes in v3:
time: 74.7 us; the launch traced here: 74.6 us
  Pallas kernels  73.3 us (98%)
    pallas_call x1, Pallas kernels, body(): pl.pallas_call(gather_kernel, out_shape=(pltpu.VMEM((count, WIDE, M), BF1...  41.6 us
    pallas_call x1, Pallas kernels, body(): pl.pallas_call(gradient_kernel, out_shape=jax.ShapeDtypeStruct((3, NV //...  16.8 us
    pallas_call x1, Pallas kernels, body(): pl.pallas_call(panel_kernel, out_shape=(jax.ShapeDtypeStruct((count, FUNC...  14.8 us

profile of v3, /device:TPU:1, one launch (start us, length us, event | category | flops | bytes accessed | tf_op | source)
XLA Modules:
  0.0 74.6 jit_solution(6957353136982046521)
XLA Ops:
  0.6 0.0 copy-start
  0.6 41.6 %shard_map.77 = (bf16[16,512,1536]{2,1,0:T(8,128)(2,1)S(1)}, bf16[4,32,384,128]{3,2,1,0:T(8,128)(2,1)S(1)}) custom-call(bf16[3,98304]{1,0:T(4,128)(2,1)} %x.1, bf16[16,384,1536]{2,1,0:T(8,128)(2,1)} %panels.1, s32[16,4,16]{2,1,0:T(4,128)} %mask_in.1, f32[16,384]{1,0:T(8,128)} %terms_in.1), custom_call_target="tpu_custom_call" | custom-call | tf_op jit(solution)/shard_map/pallas_call | solution.py:340
  42.3 0.0 copy-done
  42.3 0.0 copy-start.1
  42.3 14.8 %shard_map.78 = (bf16[16,384,384]{2,1,0:T(8,128)(2,1)}, f32[384,128]{1,0:T(8,128)S(1)}) custom-call(bf16[4,32,384,128]{3,2,1,0:T(8,128)(2,1)S(1)} %get-tuple-element.6.rot, bf16[16,512,1536]{2,1,0:T(8,128)(2,1)S(1)} %get-tuple-element.7.pext, s32[16,16]{1,0:T(8,128)S(1)} %copy-done), custom_call_target="tpu_custom_call" | custom-call | flops 9699999744 | bytes 5000000 | tf_op jit(solution)/shard_map/pallas_call | solution.py:364
  57.1 0.0 copy-done.1
  57.1 16.8 %shard_map.79 = f32[3,16,128]{2,1,0:T(8,128)S(1)} custom-call(f32[384,128]{1,0:T(8,128)S(1)} %get-tuple-element.9.sums, s32[4,16]{1,0:T(4,128)S(1)} %bitcast.6), custom_call_target="tpu_custom_call" | custom-call | tf_op jit(solution)/shard_map/pallas_call | solution.py:376
  74.0 0.6 copy.10
Async XLA Ops:
  0.6 41.7 %copy-start = (s32[16,16]{1,0:T(8,128)S(1)}, s32[16,16]{1,0:T(8,128)}, u32[]{:S(2)}) copy-start(s32[16,16]{1,0:T(8,128)} %conn.1) | copy-start | bytes 3076
  42.3 14.8 %copy-start.1 = (s32[16,4]{0,1:T(4,128)S(1)}, s32[16,4]{0,1:T(4,128)}, u32[]{:S(2)}) copy-start(s32[16,4]{0,1:T(4,128)} %param.10) | copy-start | bytes 772

commit v4 on v3

--- a/solution.py
+++ b/solution.py
@@ -23,8 +23,8 @@
 LIMIT_A = 12
 LIMIT_B = 12
 CHUNKS = 2
-EARLY = 4
-APART = 6
+EARLY = 2
+APART = 7
 UNROLL = 4
 PART = COLS // CHUNKS
 HALF = ROWS // 2
@@ -164,13 +164,13 @@
                     rot[r, q * (PART // NB) + g * 4 + u, rows, :] = turned.astype(BF16)
 
     for q in range(CHUNKS):
+        if q:
+            relay(q - 1)
         pack(q)
         for c in sends(q):
             c.start()
         if q == 0:
             pl.loop(done, count)(prepare)
-        if q:
-            relay(q - 1)
         rotate(z, q)
     relay(CHUNKS - 1)
     for q in range(CHUNKS):

time: 74.7 us -> 72.8 us (0.975)
  Pallas kernels: 73.3 us -> 71.3 us
    pallas_call x1, Pallas kernels: 16.8 us -> 14.6 us  [body(): pl.pallas_call(gradient_kernel, out_shape=jax.ShapeDtypeStruct((3, NV //...]
where the time goes in v4:
time: 72.8 us; the launch traced here: 72.7 us
  Pallas kernels  71.3 us (98%)
    pallas_call x1, Pallas kernels, body(): pl.pallas_call(gather_kernel, out_shape=(pltpu.VMEM((count, WIDE, M), BF1...  41.9 us
    pallas_call x1, Pallas kernels, body(): pl.pallas_call(panel_kernel, out_shape=(jax.ShapeDtypeStruct((count, FUNC...  14.8 us
    pallas_call x1, Pallas kernels, body(): pl.pallas_call(gradient_kernel, out_shape=jax.ShapeDtypeStruct((3, NV //...  14.6 us

profile of v4, /device:TPU:1, one launch (start us, length us, event | category | flops | bytes accessed | tf_op | source)
XLA Modules:
  0.0 72.7 jit_solution(263257609557373987)
XLA Ops:
  0.6 0.0 copy-start
  0.6 41.9 %shard_map.77 = (bf16[16,512,1536]{2,1,0:T(8,128)(2,1)S(1)}, bf16[4,32,384,128]{3,2,1,0:T(8,128)(2,1)S(1)}) custom-call(bf16[3,98304]{1,0:T(4,128)(2,1)} %x.1, bf16[16,384,1536]{2,1,0:T(8,128)(2,1)} %panels.1, s32[16,4,16]{2,1,0:T(4,128)} %mask_in.1, f32[16,384]{1,0:T(8,128)} %terms_in.1), custom_call_target="tpu_custom_call" | custom-call | tf_op jit(solution)/shard_map/pallas_call | solution.py:340
  42.6 0.0 copy-done
  42.6 0.0 copy-start.1
  42.6 14.8 %shard_map.78 = (bf16[16,384,384]{2,1,0:T(8,128)(2,1)}, f32[384,128]{1,0:T(8,128)S(1)}) custom-call(bf16[4,32,384,128]{3,2,1,0:T(8,128)(2,1)S(1)} %get-tuple-element.6.rot, bf16[16,512,1536]{2,1,0:T(8,128)(2,1)S(1)} %get-tuple-element.7.pext, s32[16,16]{1,0:T(8,128)S(1)} %copy-done), custom_call_target="tpu_custom_call" | custom-call | flops 9699999744 | bytes 5000000 | tf_op jit(solution)/shard_map/pallas_call | solution.py:364
  57.4 0.0 copy-done.1
  57.4 14.6 %shard_map.79 = f32[3,16,128]{2,1,0:T(8,128)S(1)} custom-call(f32[384,128]{1,0:T(8,128)S(1)} %get-tuple-element.9.sums, s32[4,16]{1,0:T(4,128)S(1)} %bitcast.6), custom_call_target="tpu_custom_call" | custom-call | tf_op jit(solution)/shard_map/pallas_call | solution.py:376
  72.0 0.6 copy.10
Async XLA Ops:
  0.6 41.9 %copy-start = (s32[16,16]{1,0:T(8,128)S(1)}, s32[16,16]{1,0:T(8,128)}, u32[]{:S(2)}) copy-start(s32[16,16]{1,0:T(8,128)} %conn.1) | copy-start | bytes 3076
  42.6 14.8 %copy-start.1 = (s32[16,4]{0,1:T(4,128)S(1)}, s32[16,4]{0,1:T(4,128)}, u32[]{:S(2)}) copy-start(s32[16,4]{0,1:T(4,128)} %param.10) | copy-start | bytes 772
